TPU v7x, 512 devices: a whole 4x8x8 slice. The times are simulated.
512 devices in a mesh: donor: 16 (over x, y_lo), gene: 32 (over z, y_hi, core).
Axes of the slice: x: 4, y: 8 (y_hi: 2, y_lo: 4; y = y_hi * 4 + y_lo), z: 8, core: 2. Of those that a mesh axis runs over, the one named last changes fastest.
Arguments:
- partition_tallies: bfloat16 [16384, 40352], P('donor', 'gene'), may hold values from 0 to 4
- blank_tallies: bfloat16 [4096, 40352], P('donor', 'gene'), may hold values from 0 to 1
- cluster_assignment: int32 [16384], P('donor'), may hold values from 0 to 63
- partition_person_label: int32 [16384], P('donor'), may hold values from 0 to 11
- person_blank_members: int32 [12, 384], replicated, may hold values from 0 to 4095
- spillover_fraction: float32 [16384], P('donor'), may hold values from 0.05 to 0.7
- cluster_expression: float32 [64, 40352], P(None, 'gene'), may hold values from 0.05 to 20
- background_profile: float32 [12, 40352], P(None, 'gene'), may hold values from 0.05 to 20
Outputs:
- new_profiles: float32 [64, 40352], P('donor', 'gene')
- new_ambient: float32 [12, 40352], P(None, 'gene')
- new_theta: float32 [16384], P('donor')
- ambient_reads: float32 [16384], P('donor')
Inputs may be any that keep to these rules, and one draw needn't show every extreme that they name: `person_blank_members`: an index may be listed more than once.
All inputs are finite; a program needn't handle non-finite values.
Results may differ from a plain program's by a relative error of at most 0.0003.
Values sent between devices are 32-bit elements; how exact they have to be, the bound alone decides.
A program may use at most 64 MiB of HBM per device.

v0:
```python
import jax
import jax.numpy as jnp
from jax import lax
from jax.sharding import PartitionSpec as P

TRANSCRIPT_TOTAL = 40352


pseudo_count = 0.5
beta_prior = 10.0
contract_rows = (((0,), (0,)), ((), ()))


def copy_for_each(value, axis):
    devices = lax.axis_size(axis)
    return lax.all_to_all(
        jnp.broadcast_to(value[None], (devices, *value.shape)), axis, 0, 0, tiled=True
    )


def of_everyone(value, axis):
    everything = copy_for_each(value, axis)
    return jnp.sum(everything, axis=0)


def packed_total(arrays, axis):
    ravelled, at, done = (jnp.concatenate([a.reshape(-1) for a in arrays]), 0, [])
    subtotal = of_everyone(ravelled, axis)
    for a in arrays:
        done.append(subtotal[at : at + a.size].reshape(a.shape))
        at += a.size
    return tuple(done)


def in_blocks(value, dim, devices):
    before, after = (value.shape[:dim], value.shape[dim + 1 :])
    return jnp.moveaxis(value.reshape(*before, devices, -1, *after), dim, 0)


def sent_and_summed(value, axis, dim):
    devices = lax.axis_size(axis)
    tiles = lax.all_to_all(in_blocks(value, dim, devices), axis, 0, 0, tiled=True)
    return jnp.sum(tiles, axis=0)


def side_by_side(arrays, axis, dim, along):
    columns = [a.reshape(*a.shape[:along], -1) for a in arrays]
    both = jnp.concatenate(columns, axis=along)
    result, at, done = (sent_and_summed(both, axis, dim), 0, [])
    for a, column in zip(arrays, columns):
        piece = result[..., at : at + column.shape[along]]
        done.append(piece.reshape(*piece.shape[:along], *a.shape[along:]))
        at += column.shape[along]
    return tuple(done)


def body(
    partition_tallies,
    blank_tallies,
    cluster_assignment,
    partition_person_label,
    person_blank_members,
    spillover_fraction,
    cluster_expression,
    background_profile,
):
    pop_count = cluster_expression.shape[0]
    donor_total = background_profile.shape[0]
    pop_hot = (
        cluster_assignment[:, None] == jnp.arange(pop_count, dtype=jnp.int32)[None, :]
    ).astype(jnp.float32)
    donor_hot = (
        partition_person_label[:, None] == jnp.arange(donor_total, dtype=jnp.int32)[None, :]
    ).astype(jnp.float32)
    looked_native = jnp.dot(pop_hot, cluster_expression, precision=lax.Precision.HIGHEST)
    looked_ambient = jnp.dot(donor_hot, background_profile, precision=lax.Precision.HIGHEST)
    theta_column = spillover_fraction[:, None]
    weight_native = (1.0 - theta_column) * looked_native
    weight_contam = theta_column * looked_ambient
    resp_native = weight_native / (weight_native + weight_contam)
    count_values = partition_tallies.astype(jnp.float32)
    native = (count_values * resp_native).astype(jnp.bfloat16)
    contam = (count_values * (1.0 - resp_native)).astype(jnp.bfloat16)
    native_part = jnp.sum(native.astype(jnp.float32), axis=1)
    contam_part = jnp.sum(contam.astype(jnp.float32), axis=1)
    blank_partition_lines = blank_tallies.shape[0]
    local_index = lax.axis_index("donor") * blank_partition_lines + jnp.arange(
        blank_partition_lines, dtype=jnp.int32
    )
    gathered_blank_tallies = jnp.sum(
        (person_blank_members[:, :, None] == local_index[None, None, :]).astype(jnp.int32), axis=1
    )
    pop_part = lax.dot_general(
        pop_hot.astype(jnp.bfloat16), native, contract_rows, preferred_element_type=jnp.float32
    )
    ambient_part = lax.dot_general(
        donor_hot.astype(jnp.bfloat16), contam, contract_rows, preferred_element_type=jnp.float32
    )
    ambient_part = ambient_part + jnp.dot(
        gathered_blank_tallies.astype(jnp.bfloat16),
        blank_tallies,
        preferred_element_type=jnp.float32,
    )
    empty_part = jnp.sum(blank_tallies.astype(jnp.float32), axis=1)
    native_reads, contam_reads, empty_reads = packed_total(
        (native_part, contam_part, empty_part), "gene"
    )
    pop_tpart = lax.dot_general(
        pop_hot, native_reads, contract_rows, precision=lax.Precision.HIGHEST
    )
    ambient_tpart = lax.dot_general(
        donor_hot, contam_reads, contract_rows, precision=lax.Precision.HIGHEST
    )
    ambient_tpart = ambient_tpart + jnp.dot(
        gathered_blank_tallies.astype(jnp.float32), empty_reads, precision=lax.Precision.HIGHEST
    )
    pop_sums, pop_total = side_by_side((pop_part, pop_tpart), "donor", 0, 1)
    background_transcript_totals, ambient_total = packed_total(
        (ambient_part, ambient_tpart), "donor"
    )
    new_profiles = (
        TRANSCRIPT_TOTAL
        * (pop_sums + pseudo_count)
        / (pop_total[:, None] + TRANSCRIPT_TOTAL * pseudo_count)
    )
    new_ambient = (
        TRANSCRIPT_TOTAL
        * (background_transcript_totals + pseudo_count)
        / (ambient_total[:, None] + TRANSCRIPT_TOTAL * pseudo_count)
    )
    new_theta = (contam_reads + beta_prior) / (native_reads + contam_reads + 2.0 * beta_prior)
    ambient_reads = contam_reads / TRANSCRIPT_TOTAL
    return (new_profiles, new_ambient, new_theta, ambient_reads)


def solution(mesh):
    in_specs = (
        P("donor", "gene"),
        P("donor", "gene"),
        P("donor"),
        P("donor"),
        P(),
        P("donor"),
        P(None, "gene"),
        P(None, "gene"),
    )
    out_specs = (P("donor", "gene"), P(None, "gene"), P("donor"), P("donor"))
    return jax.shard_map(body, mesh=mesh, in_specs=in_specs, out_specs=out_specs, check_vma=False)
```

profile of v0, /device:TPU:1, one launch (start us, length us, event | category | flops | bytes accessed | tf_op | source)
XLA Modules:
  0.0 98.1 jit_solution(5155986429318402895)
XLA Ops:
  0.6 0.0 copy-start
  0.6 0.0 copy-start.4
  0.7 0.0 copy-start.3
  0.7 0.0 copy-start.1
  0.7 1.4 %convert_reduce_fusion.3 = f32[256]{0:T(256)S(1)} fusion(bf16[256,1261]{0,1:T(8,128)(2,1)} %param.9), kind=kLoop, calls=%fused_computation.9 | loop fusion | flops 645376 | bytes 646656 | tf_op jit(solution)/shard_map/reduce_sum | solution.py:104
  2.1 0.7 broadcast_subtract_fusion
  2.8 3.2 %fusion.3 = f32[1024,1261]{0,1:T(8,128)S(1)} fusion(f32[12,1261]{1,0:T(8,128)} %param.15, s32[1024]{0:T(1024)} %param.11), kind=kOutput, calls=%fused_computation.15 | convolution fusion | flops 185954304 | bytes 5229680 | tf_op jit(solution)/shard_map/dot_general | solution.py:76
  6.0 0.0 copy-done
  6.0 0.0 copy-done.4
  6.0 0.0 copy-done.3
  6.0 0.0 copy-done.1
  6.1 6.3 %convert_reduce_fusion.1 = (f32[1024]{0:T(1024)S(1)}, f32[1024]{0:T(1024)S(1)}, f32[1024,1261]{0,1:T(8,128)}) fusion(bf16[1024,1261]{0,1:T(8,128)(2,1)S(1)} %copy-done.1, f32[1024,1261]{0,1:T(8,128)S(1)} %fusion.3, f32[1024]{0:T(1024)S(1)} %copy-done.4, f32[64,1261]{1,0:T(8,128)S(1)} %copy-done, s32[1024]{0:T(1024)S(1)} %copy-done.3, ...), kind=kOutput, calls=%fused_computation.6 | convolution fusion | flops 1009831936 | bytes 13255936 | tf_op jit(solution)/shard_map/dot_general | solution.py:75
  12.4 0.9 broadcast_in_dim.4
  13.3 17.2 %all-to-all-start = ((f32[32,1,2304]{2,1,0:T(1,128)}), f32[32,1,2304]{2,1,0:T(1,128)S(1)}, u32[]{:S(2)}, u32[]{:S(2)}) async-start(f32[32,1,2304]{2,1,0:T(1,128)} %broadcast_in_dim.4), calls=%async_computation | async-start | bytes 589824 | tf_op jit(solution)/shard_map/all_to_all | solution.py:16
  30.5 0.6 iota_add_fusion
  31.1 3.5 %fusion.5 = f32[64,1261]{1,0:T(8,128)S(1)} fusion(s32[1024]{0:T(1024)S(1)} %copy-done.3, f32[1024,1261]{0,1:T(8,128)} %get-tuple-element.10, bf16[1024,1261]{0,1:T(8,128)(2,1)S(1)} %copy-done.1), kind=kOutput, calls=%fused_computation.20 | convolution fusion | flops 169352192 | bytes 8074496 | tf_op jit(solution)/shard_map/dot_general | solution.py:93
  34.6 0.8 concatenate.14
  35.5 0.0 copy-start.2
  35.5 2.1 %convert_reduce_fusion.2 = s32[12,256]{1,0:T(8,128)S(1)} fusion(s32[256]{0:T(256)} %iota_add_fusion, s32[12,384]{1,0:T(8,128)} %param.12), kind=kLoop, calls=%fused_computation.7 | loop fusion | flops 3535872 | bytes 31744 | tf_op jit(solution)/shard_map/reduce_sum | solution.py:90
  37.5 4.1 %fusion.6 = f32[12,1261]{1,0:T(8,128)} fusion(s32[1024]{0:T(1024)} %param.11, bf16[1024,1261]{0,1:T(8,128)(2,1)S(1)} %copy-done.1, f32[1024,1261]{0,1:T(8,128)} %get-tuple-element.10), kind=kOutput, calls=%fused_computation.21 | convolution fusion | flops 36192256 | bytes 7812208 | tf_op jit(solution)/shard_map/dot_general | solution.py:96
  41.6 2.8 %all-to-all-done = f32[32,1,2304]{2,1,0:T(1,128)S(1)} async-done(((f32[32,1,2304]{2,1,0:T(1,128)}), f32[32,1,2304]{2,1,0:T(1,128)S(1)}, u32[]{:S(2)}, u32[]{:S(2)}) %all-to-all-start) | async-done | bytes 294944 | tf_op jit(solution)/shard_map/all_to_all | solution.py:16
  44.5 0.2 reduce_sum.66
  44.6 0.6 broadcast_multiply_fusion
  45.2 1.4 %fusion.4 = f32[1,64]{0,1:T(8,128)S(1)} fusion(f32[1024,1]{0,1:T(1,128)S(1)} %bitcast.20, s32[1024]{0:T(1024)} %param.10), kind=kOutput, calls=%fused_computation.18 | convolution fusion | flops 851968 | bytes 8448 | tf_op jit(solution)/shard_map/dot_general | solution.py:108
  46.7 0.0 copy-done.2
  46.7 0.8 pad_maximum_fusion
  47.5 7.4 %all-to-all-start.1 = ((f32[16,4,1262]{2,1,0:T(4,128)}), f32[16,4,1262]{2,1,0:T(4,128)S(1)}, u32[]{:S(2)}, u32[]{:S(2)}) async-start(f32[16,4,1262]{2,1,0:T(4,128)} %pad_maximum_fusion), calls=%async_computation.1 | async-start | bytes 655360 | tf_op jit(solution)/shard_map/all_to_all | solution.py:42
  54.9 1.4 %convolution_add_fusion = f32[12,1261]{1,0:T(8,128)S(1)} fusion(f32[12,1261]{1,0:T(8,128)} %fusion.6, bf16[256,1261]{0,1:T(8,128)(2,1)} %param.9, s32[12,256]{1,0:T(8,128)S(1)} %convert_reduce_fusion.2), kind=kOutput, calls=%fused_computation.8 | convolution fusion | flops 7765788 | bytes 778976 | tf_op jit(solution)/shard_map/dot_general | solution.py:99
  56.2 0.1 reshape.45
  56.4 1.1 %convolution_bitcast_fusion.1 = f32[12]{0:T(128)S(1)} fusion(f32[1024,1]{0,1:T(1,128)S(1)} %bitcast.19, s32[1024]{0:T(1024)} %param.11), kind=kOutput, calls=%fused_computation.12 | convolution fusion | flops 159744 | bytes 8240 | tf_op jit(solution)/shard_map/dot_general | solution.py:111
  57.4 0.1 fusion.2
  57.6 0.1 pad_maximum_fusion.1
  57.7 8.5 %all-to-all-done.1 = f32[16,4,1262]{2,1,0:T(4,128)S(1)} async-done(((f32[16,4,1262]{2,1,0:T(4,128)}), f32[16,4,1262]{2,1,0:T(4,128)S(1)}, u32[]{:S(2)}, u32[]{:S(2)}) %all-to-all-start.1) | async-done | bytes 323104 | tf_op jit(solution)/shard_map/all_to_all | solution.py:42
  66.1 1.5 %broadcast_in_dim.5 = f32[16,1,15144]{2,1,0:T(1,128)} broadcast(f32[15144]{0:T(1024)S(1)} %pad_maximum_fusion.1), dimensions={2} | broadcast | bytes 1029792 | tf_op jit(solution)/shard_map/broadcast_in_dim | solution.py:17
  67.6 3.6 %all-to-all-start.2 = ((f32[16,1,15144]{2,1,0:T(1,128)}), f32[16,1,15144]{2,1,0:T(1,128)S(1)}, u32[]{:S(2)}, u32[]{:S(2)}) async-start(f32[16,1,15144]{2,1,0:T(1,128)} %broadcast_in_dim.5), calls=%async_computation.2 | async-start | bytes 1949696 | tf_op jit(solution)/shard_map/all_to_all | solution.py:16
  71.2 0.1 reduce_sum.67
  71.3 0.2 fusion.18
  71.5 0.7 fusion.15
  72.2 24.4 %all-to-all-done.2 = f32[16,1,15144]{2,1,0:T(1,128)S(1)} async-done(((f32[16,1,15144]{2,1,0:T(1,128)}), f32[16,1,15144]{2,1,0:T(1,128)S(1)}, u32[]{:S(2)}, u32[]{:S(2)}) %all-to-all-start.2) | async-done | bytes 969248 | tf_op jit(solution)/shard_map/all_to_all | solution.py:16
  96.6 0.6 reduce_sum.69
  97.2 0.1 slice_add_fusion.3
  97.3 0.1 mul.51
  97.4 0.7 broadcast_divide_fusion
  (3 shorter events, 0.0 us)
Async XLA Ops:
  0.6 5.4 %copy-start = (f32[64,1261]{1,0:T(8,128)S(1)}, f32[64,1261]{1,0:T(8,128)}, u32[]{:S(2)}) copy-start(f32[64,1261]{1,0:T(8,128)} %param.14) | copy-start | bytes 968452
  0.6 5.4 %copy-start.4 = (f32[1024]{0:T(1024)S(1)}, f32[1024]{0:T(1024)}, u32[]{:S(2)}) copy-start(f32[1024]{0:T(1024)} %param.13) | copy-start | bytes 12292
  0.7 5.4 %copy-start.3 = (s32[1024]{0:T(1024)S(1)}, s32[1024]{0:T(1024)}, u32[]{:S(2)}) copy-start(s32[1024]{0:T(1024)} %param.10) | copy-start | bytes 12292
  0.7 5.4 %copy-start.1 = (bf16[1024,1261]{0,1:T(8,128)(2,1)S(1)}, bf16[1024,1261]{0,1:T(8,128)(2,1)}, u32[]{:S(2)}) copy-start(bf16[1024,1261]{0,1:T(8,128)(2,1)} %param.8) | copy-start | bytes 7747588
  13.3 31.2 %all-to-all-start = ((f32[32,1,2304]{2,1,0:T(1,128)}), f32[32,1,2304]{2,1,0:T(1,128)S(1)}, u32[]{:S(2)}, u32[]{:S(2)}) async-start(f32[32,1,2304]{2,1,0:T(1,128)} %broadcast_in_dim.4), calls=%async_computation | async-start | bytes 589824 | tf_op jit(solution)/shard_map/all_to_all | solution.py:16
  35.5 11.2 %copy-start.2 = (f32[16,4,1261]{2,1,0:T(4,128)S(1)}, f32[16,4,1261]{2,1,0:T(4,128)}, u32[]{:S(2)}) copy-start(f32[16,4,1261]{2,1,0:T(4,128)} %concatenate.14) | copy-start | bytes 968452
  47.5 18.7 %all-to-all-start.1 = ((f32[16,4,1262]{2,1,0:T(4,128)}), f32[16,4,1262]{2,1,0:T(4,128)S(1)}, u32[]{:S(2)}, u32[]{:S(2)}) async-start(f32[16,4,1262]{2,1,0:T(4,128)} %pad_maximum_fusion), calls=%async_computation.1 | async-start | bytes 655360 | tf_op jit(solution)/shard_map/all_to_all | solution.py:42
  67.6 29.0 %all-to-all-start.2 = ((f32[16,1,15144]{2,1,0:T(1,128)}), f32[16,1,15144]{2,1,0:T(1,128)S(1)}, u32[]{:S(2)}, u32[]{:S(2)}) async-start(f32[16,1,15144]{2,1,0:T(1,128)} %broadcast_in_dim.5), calls=%async_computation.2 | async-start | bytes 1949696 | tf_op jit(solution)/shard_map/all_to_all | solution.py:16
where the time goes:
time: 98.7 us; the launch traced here: 98.1 us
  waiting for transfers between devices  35.7 us (36%)
  starting transfers between devices  28.3 us (29%)
  matrix products  21.2 us (21%)
  other arithmetic  8.75 us (9%)
  local copies, waits for them, and re-layouts  3.42 us (3%)
    all_to_all x2, waiting for transfers between devices, copy_for_each(): lax.all_to_all(jnp.broadcast_to(value[None], (devices, *value.shape)), ax...  27.2 us
    all_to_all x2, starting transfers between devices, copy_for_each(): lax.all_to_all(jnp.broadcast_to(value[None], (devices, *value.shape)), ax...  20.9 us
    all_to_all x1, waiting for transfers between devices, sent_and_summed(): lax.all_to_all(in_blocks(value, dim, devices), axis, 0, 0, tiled=True)  8.45 us
    all_to_all x1, starting transfers between devices, sent_and_summed(): lax.all_to_all(in_blocks(value, dim, devices), axis, 0, 0, tiled=True)  7.37 us
    dot_general x1, matrix products, body(): jnp.dot(pop_hot, cluster_expression, precision=lax.Precision.HIGHEST)  6.35 us
    dot_general x1, matrix products, body(): lax.dot_general(donor_hot.astype(jnp.bfloat16), contam, contract_rows, pr...  4.08 us
    dot_general x1, matrix products, body(): lax.dot_general(pop_hot.astype(jnp.bfloat16), native, contract_rows, pref...  3.5 us
    dot_general x1, matrix products, body(): jnp.dot(donor_hot, background_profile, precision=lax.Precision.HIGHEST)  3.22 us
  transfers between devices with their start and end apart: 3, of which 3 were waited for; matrix products, arithmetic and copies ran while one was open for 15% of the time, Pallas kernels for 0%

commit v1 on v0

v1 whole, which is shorter than its diff:
```python
import jax
import jax.numpy as jnp
from jax import lax
from jax.experimental import pallas as pl
from jax.experimental.pallas import tpu as pltpu
from jax.sharding import PartitionSpec as P

TOTAL = 40352
PSEUDO = 0.5
BETA = 10.0
G, N, NB, GP = 1261, 1024, 256, 1280
POPS, DONORS = 64, 12
CHUNK = 256
EARLY = 24
ROWS = 48
f32, bf16 = jnp.float32, jnp.bfloat16
MESH = pl.DeviceIdType.MESH
LAST = (((1,), (1,)), ((), ()))
FIRST = (((0,), (0,)), ((), ()))


def thirds(v):
    hi = v.astype(bf16)
    rest = v - hi.astype(f32)
    mid = rest.astype(bf16)
    return hi, mid, (rest - mid.astype(f32)).astype(bf16)


def hot(mask):
    return jnp.where(mask, 1.0, 0.0).astype(bf16)


def padded_tail(ref):
    width = ref.shape[1]
    ragged = jnp.concatenate([ref[1248:G].astype(f32), jnp.zeros((3, width), f32)], axis=0)
    return jnp.concatenate([ref[1024:1248], ragged.astype(bf16), jnp.zeros((16, width), bf16)], axis=0)


def kernel(
    x_hbm, b_hbm, lab_hbm, don_hbm, mem_hbm, th_hbm, e_hbm, p_hbm,
    prof_ref, amb_ref, theta_ref, reads_ref,
    xs, bs, lab_v, don_v, mem_v, th_v, e_v, p_v, hots, table,
    send, got, mine, from_core, gene_out, gene_in, final_out, final_in, amb_all, tot_out, tot_in,
    in_sem, s_sem, r_sem,
):
    d = lax.axis_index("donor")
    q = lax.axis_index("gene")
    core = lax.rem(q, 2)
    other = {"gene": q + 1 - 2 * core}

    smalls = (
        (lab_hbm, lab_v), (don_hbm, don_v), (th_hbm, th_v), (e_hbm, e_v), (p_hbm, p_v), (mem_hbm, mem_v),
    )
    small_in = [pltpu.make_async_copy(a, b, in_sem.at[i]) for i, (a, b) in enumerate(smalls)]
    for c in small_in:
        c.start()
    x_in = []
    for c in range(5):
        rows = pl.ds(CHUNK * c, min(CHUNK, G - CHUNK * c))
        x_in.append(pltpu.make_async_copy(x_hbm.at[rows], xs.at[rows], in_sem.at[6 + c]))
    b_in = pltpu.make_async_copy(b_hbm, bs, in_sem.at[11])
    for c in x_in[:1] + [b_in] + x_in[1:]:
        c.start()

    barrier = pltpu.get_barrier_semaphore()

    def greet(j, carry):
        pl.semaphore_signal(barrier, inc=1, device_id={"donor": lax.rem(d + j, 16)}, device_id_type=MESH)
        pl.semaphore_signal(barrier, inc=1, device_id={"gene": lax.rem(q + 2 * j, 32)}, device_id_type=MESH)
        return carry

    lax.fori_loop(1, 16, greet, 0)
    pl.semaphore_signal(barrier, inc=1, device_id=other, device_id_type=MESH)

    for c in small_in:
        c.wait()
    labels, people, theta = lab_v[...], don_v[...], th_v[...]
    pop_hot = hot(labels == lax.broadcasted_iota(jnp.int32, (POPS, N), 0))
    donor_hot = hot(people == lax.broadcasted_iota(jnp.int32, (16, N), 0))
    for i in range(3):
        hots[64 * i : 64 * i + 64] = pop_hot
        hots[192 + 16 * i : 208 + 16 * i] = donor_hot
    row = lax.broadcasted_iota(jnp.int32, (16, N), 0)
    odds = jnp.zeros((16, N), f32)
    for i, v in enumerate(thirds((jnp.log(theta) - jnp.log(1.0 - theta)) * -0.5)):
        odds = jnp.where(row == i, v.astype(f32), odds)
    hots[240:256] = odds.astype(bf16)
    for i, v in enumerate(thirds(jnp.log(e_v[...]) * 0.5)):
        table[64 * i : 64 * i + 64, 0:G] = v
    log_ambient = jnp.concatenate([jnp.log(p_v[...]) * -0.5, jnp.zeros((4, G), f32)], axis=0)
    for i, v in enumerate(thirds(log_ambient)):
        table[192 + 16 * i : 208 + 16 * i, 0:G] = v
    table[240:256] = hot(lax.broadcasted_iota(jnp.int32, (16, GP), 0) < 3)
    table[0:240, G:GP] = jnp.zeros((240, GP - G), bf16)

    members = mem_v[...] - d * NB
    empties = lax.broadcasted_iota(jnp.int32, (NB, 128), 0)
    lane = lax.broadcasted_iota(jnp.int32, (128, 128), 1)
    listed = jnp.zeros((NB, 128), f32)
    for r in range(DONORS):
        count = jnp.zeros((NB, 128), f32)
        for t in range(3):
            count = count + jnp.where(members[r : r + 1, 128 * t : 128 * t + 128] == empties, 1.0, 0.0)
        listed = listed + jnp.dot(count.astype(bf16), hot(lane == POPS + r), preferred_element_type=f32)
    listed_hi = listed.astype(bf16)
    listed_lo = (listed - listed_hi.astype(f32)).astype(bf16)

    pops = jnp.concatenate([pop_hot, jnp.zeros((64, N), bf16)], axis=0)
    folk = jnp.concatenate([jnp.zeros((64, N), bf16), donor_hot, jnp.zeros((48, N), bf16)], axis=0)
    send[15, 40:48] = jnp.zeros((8, 128), f32)

    native_acc = jnp.zeros((8, N), f32)
    contam_acc = jnp.zeros((8, N), f32)
    totals = jnp.zeros((8, 128), f32)

    def spread(first, count, index):
        def one(j, carry):
            peer = lax.rem(d + j, 16)
            pltpu.make_async_remote_copy(
                send.at[peer, pl.ds(first, count)], got.at[j - 1, pl.ds(first, count)],
                s_sem.at[index], r_sem.at[index], device_id={"donor": peer}, device_id_type=MESH,
            ).start()
            return carry

        lax.fori_loop(1, 16, one, 0)

    for c in range(5):
        log_odds = lax.dot_general(table[:, CHUNK * c : CHUNK * c + CHUNK], hots[...], FIRST, preferred_element_type=f32)
        x_in[c].wait()
        if c == 0:
            b_in.wait()
        if c < 4:
            counts, blanks = xs[CHUNK * c : CHUNK * c + CHUNK], bs[CHUNK * c : CHUNK * c + CHUNK]
        else:
            counts, blanks = padded_tail(xs), padded_tail(bs)
        half = counts.astype(f32) * 0.5
        swing = half * jnp.tanh(log_odds)
        native = (half + swing).astype(bf16)
        contam = (half - swing).astype(bf16)
        native_acc = native_acc + jnp.sum(native.astype(f32).reshape(CHUNK // 8, 8, N), axis=0)
        contam_acc = contam_acc + jnp.sum(contam.astype(f32).reshape(CHUNK // 8, 8, N), axis=0)
        sums = lax.dot_general(native, pops, LAST, preferred_element_type=f32)
        sums = sums + lax.dot_general(contam, folk, LAST, preferred_element_type=f32)
        sums = sums + jnp.dot(blanks, listed_hi, preferred_element_type=f32)
        sums = sums + jnp.dot(blanks, listed_lo, preferred_element_type=f32)
        totals = totals + jnp.sum(sums.reshape(CHUNK // 8, 8, 128), axis=0)
        for h in range(2):
            t = 2 * c + h
            turned = sums[128 * h : 128 * h + 128].T
            for i in range(16):
                send[i, 4 * t : 4 * t + 4] = turned[4 * i : 4 * i + 4]
            r = 0
            while r < DONORS:
                u = 12 * t + r
                run = min(DONORS - r, 8 - u % 8)
                send[u // 8, 40 + u % 8 : 40 + u % 8 + run] = turned[64 + r : 64 + r + run]
                r += run
        if c == 2:
            pl.semaphore_wait(barrier, 31)
            spread(0, EARLY, 0)

    native_row = jnp.sum(native_acc, axis=0, keepdims=True)
    contam_row = jnp.sum(contam_acc, axis=0, keepdims=True)
    for i in range(8):
        mine[i : i + 1] = native_row[:, 128 * i : 128 * i + 128]
        mine[16 + i : 17 + i] = contam_row[:, 128 * i : 128 * i + 128]
    mine[8:16] = totals
    to_core = pltpu.make_async_remote_copy(
        mine.at[pl.ds(8 - 8 * core, 16)], from_core, s_sem.at[2], r_sem.at[2], device_id=other, device_id_type=MESH
    )
    to_core.start()
    spread(EARLY, ROWS - EARLY, 1)

    to_core.wait_recv()
    at_reads = pl.multiple_of(8 * core, 8)
    at_total = pl.multiple_of(8 - 8 * core, 8)
    gene_out[0:8] = mine[pl.ds(pl.multiple_of(16 * core, 8), 8)] + from_core[pl.ds(at_reads, 8)]
    gene_out[8:16] = mine[8:16] + from_core[pl.ds(at_total, 8)]

    def to_gene(j, carry):
        pltpu.make_async_remote_copy(
            gene_out, gene_in.at[j - 1], s_sem.at[3], r_sem.at[3],
            device_id={"gene": lax.rem(q + 2 * j, 32)}, device_id_type=MESH,
        ).start()
        return carry

    lax.fori_loop(1, 16, to_gene, 0)

    def wait_for(ref, sem):
        pltpu.make_async_copy(ref, ref, sem).wait()

    early, late = pl.ds(0, EARLY), pl.ds(EARLY, ROWS - EARLY)
    fifteen = pl.ds(0, 15)
    wait_for(got.at[fifteen, early], r_sem.at[0])
    wait_for(got.at[fifteen, late], r_sem.at[1])
    both = send[d] + jnp.sum(got[...], axis=0)
    amb_all[d] = both[40:48]

    def to_all(j, carry):
        pltpu.make_async_remote_copy(
            amb_all.at[d], amb_all.at[d], s_sem.at[4], r_sem.at[4],
            device_id={"donor": lax.rem(d + j, 16)}, device_id_type=MESH,
        ).start()
        return carry

    lax.fori_loop(1, 16, to_all, 0)

    wait_for(gene_in, r_sem.at[3])
    gene_sum = gene_out[...] + jnp.sum(gene_in[...], axis=0)
    tot_out[...] = gene_sum[8:16]

    def to_donors(j, carry):
        pltpu.make_async_remote_copy(
            tot_out, tot_in.at[j - 1], s_sem.at[5], r_sem.at[5],
            device_id={"donor": lax.rem(d + j, 16)}, device_id_type=MESH,
        ).start()
        return carry

    lax.fori_loop(1, 16, to_donors, 0)
    final_out[...] = gene_sum[0:8]
    swap = pltpu.make_async_remote_copy(
        final_out, final_in, s_sem.at[6], r_sem.at[6], device_id=other, device_id_type=MESH
    )
    swap.start()
    swap.wait_recv()
    ours, theirs = final_out[...], final_in[...]
    native_reads = jnp.where(core == 0, ours, theirs)
    contam_reads = jnp.where(core == 0, theirs, ours)
    theta_ref[...] = (contam_reads + BETA) / (native_reads + contam_reads + 2.0 * BETA)
    reads_ref[...] = contam_reads / TOTAL

    wait_for(amb_all.at[fifteen], r_sem.at[4])
    wait_for(tot_in, r_sem.at[5])
    total = jnp.sum(tot_out[...] + jnp.sum(tot_in[...], axis=0), axis=0, keepdims=True)

    def column(wanted, count):
        lanes = lax.broadcasted_iota(jnp.int32, (count, 128), 1)
        rows = lax.broadcasted_iota(jnp.int32, (count, 128), 0)
        return jnp.sum(jnp.where(lanes == wanted(rows), total, 0.0), axis=1, keepdims=True) + TOTAL * PSEUDO

    profile = TOTAL * (both[0:40] + PSEUDO) / column(lambda r: 4 * d + r % 4, 40)
    below = column(lambda r: POPS + r, DONORS)
    ambient = amb_all[...].reshape(128, 128)
    for t in range(10):
        width = min(128, G - 128 * t)
        prof_ref[:, 128 * t : 128 * t + width] = profile[4 * t : 4 * t + 4, 0:width]
        people_rows = TOTAL * (ambient[12 * t : 12 * t + 12] + PSEUDO) / below
        amb_ref[:, 128 * t : 128 * t + width] = people_rows[:, 0:width]

    wait_for(send.at[fifteen, early], s_sem.at[0])
    wait_for(send.at[fifteen, late], s_sem.at[1])
    to_core.wait_send()
    wait_for(gene_in, s_sem.at[3])
    wait_for(amb_all.at[fifteen], s_sem.at[4])
    wait_for(tot_in, s_sem.at[5])
    swap.wait_send()


def body(tallies, blanks, labels, people, members, theta, profiles, ambient):
    hbm = pl.BlockSpec(memory_space=pltpu.HBM)
    vmem = pl.BlockSpec(memory_space=pltpu.VMEM)
    v = pltpu.VMEM
    profile, new_ambient, new_theta, reads = pl.pallas_call(
        kernel,
        out_shape=(
            jax.ShapeDtypeStruct((4, G), f32),
            jax.ShapeDtypeStruct((DONORS, G), f32),
            jax.ShapeDtypeStruct((8, 128), f32),
            jax.ShapeDtypeStruct((8, 128), f32),
        ),
        in_specs=[hbm] * 8,
        out_specs=(vmem,) * 4,
        scratch_shapes=[
            v((G, N), bf16), v((G, NB), bf16), v((1, N), jnp.int32), v((1, N), jnp.int32),
            v((DONORS, 384), jnp.int32), v((1, N), f32), v((POPS, G), f32), v((DONORS, G), f32),
            v((256, N), bf16), v((256, GP), bf16),
            v((16, ROWS, 128), f32), v((15, ROWS, 128), f32), v((24, 128), f32), v((16, 128), f32),
            v((16, 128), f32), v((15, 16, 128), f32), v((8, 128), f32), v((8, 128), f32),
            v((16, 8, 128), f32), v((8, 128), f32), v((15, 8, 128), f32),
            pltpu.SemaphoreType.DMA((12,)), pltpu.SemaphoreType.DMA((7,)), pltpu.SemaphoreType.DMA((7,)),
        ],
        compiler_params=pltpu.CompilerParams(
            collective_id=0, has_side_effects=True, vmem_limit_bytes=56 << 20
        ),
    )(
        tallies.T, blanks.T, labels.reshape(1, N), people.reshape(1, N), members, theta.reshape(1, N),
        profiles, ambient,
    )
    return profile, new_ambient, new_theta.reshape(N), reads.reshape(N)


def solution(mesh):
    in_specs = (
        P("donor", "gene"), P("donor", "gene"), P("donor"), P("donor"), P(), P("donor"),
        P(None, "gene"), P(None, "gene"),
    )
    out_specs = (P("donor", "gene"), P(None, "gene"), P("donor"), P("donor"))
    return jax.shard_map(body, mesh=mesh, in_specs=in_specs, out_specs=out_specs, check_vma=False)
```

time: 98.7 us -> 42.2 us (0.43)
  waiting for transfers between devices: 35.7 us -> 0 us
  Pallas kernels: 0 us -> 35.6 us
  starting transfers between devices: 28.3 us -> 0 us
  matrix products: 21.2 us -> 0 us
  other arithmetic: 8.75 us -> 0 us
  local copies, waits for them, and re-layouts: 3.42 us -> 5.4 us
    all_to_all x3 -> x0, waiting for transfers between devices: 35.7 us -> none  [the longest x2 27.2 us: copy_for_each(): lax.all_to_all(jnp.broadcast_to(value[None], (devices, *value.shape)), ax...]
    pallas_call x0 -> x1, Pallas kernels: none -> 35.6 us  [body(): pl.pallas_call(kernel, out_shape=(jax.ShapeDtypeStruct((4, G), f32), jax....]
    all_to_all x3 -> x0, starting transfers between devices: 28.3 us -> none  [the longest x2 20.9 us: copy_for_each(): lax.all_to_all(jnp.broadcast_to(value[None], (devices, *value.shape)), ax...]
    dot_general x8 -> x0, matrix products: 21.2 us -> none  [the longest x1 6.35 us: body(): jnp.dot(pop_hot, cluster_expression, precision=lax.Precision.HIGHEST)]
    unnamed x10 -> x4, local copies, waits for them, and re-layouts: 0.03 us -> 5.4 us
    reduce_sum x5 -> x0, other arithmetic: 4.33 us -> none  [the longest x1 2.06 us: body(): jnp.sum((person_blank_members[:, :, None] == local_index[None, None, :])....]
    broadcast_in_dim x2 -> x0, local copies, waits for them, and re-layouts: 2.34 us -> none  [copy_for_each(): jnp.broadcast_to(value[None], (devices, *value.shape))]
    div x3 -> x0, other arithmetic: 2.01 us -> none  [the longest x1 0.72 us: body(): TRANSCRIPT_TOTAL * (background_transcript_totals + pseudo_count)]
  transfers between devices with their start and end apart: 3 -> 0, of which waited for: 3 -> 0; matrix products, arithmetic and copies ran while one was open for 15% -> 0% of each run, Pallas kernels for 0% -> 0%
where the time goes in v1:
time: 42.2 us; the launch traced here: 41.6 us
  Pallas kernels  35.6 us (84%)
  local copies, waits for them, and re-layouts  5.4 us (13%)
  between operations  0.64 us (2%)
    pallas_call x1, Pallas kernels, body(): pl.pallas_call(kernel, out_shape=(jax.ShapeDtypeStruct((4, G), f32), jax....  35.6 us
    unnamed x4, local copies, waits for them, and re-layouts  5.4 us

profile of v1, /device:TPU:1, one launch (start us, length us, event | category | flops | bytes accessed | tf_op | source)
XLA Modules:
  0.0 41.6 jit_solution(9666463157966945383)
XLA Ops:
  0.6 35.6 %shard_map.111 = (f32[4,1261]{1,0:T(4,128)}, f32[12,1261]{1,0:T(8,128)}, f32[8,128]{1,0:T(8,128)}, f32[8,128]{1,0:T(8,128)}) custom-call(bf16[1261,1024]{1,0:T(8,128)(2,1)} %bitcast.7, bf16[1261,256]{1,0:T(8,128)(2,1)} %bitcast.8, s32[1,1024]{1,0:T(1,128)} %bitcast.11, s32[1,1024]{1,0:T(1,128)} %bitcast.12, s32[12,384]{1,0:T(8,128)} %mem_hbm.1, ...), custom_call_target="tpu_custom_call" | custom-call | tf_op jit(solution)/shard_map/pallas_call | solution.py:263
  36.2 1.3 %copy.16 = f32[4,1261]{1,0:T(4,128)} copy(f32[4,1261]{1,0:T(4,128)} %get-tuple-element.16) | data formatting | bytes 40352
  37.5 1.5 %copy.17 = f32[12,1261]{1,0:T(8,128)} copy(f32[12,1261]{1,0:T(8,128)} %get-tuple-element.17) | data formatting | bytes 121056
  39.1 1.3 %copy.18 = f32[1024]{0:T(1024)} copy(f32[1024]{0:T(1024)} %bitcast.10) | data formatting | bytes 8192
  40.3 1.3 %copy.19 = f32[1024]{0:T(1024)} copy(f32[1024]{0:T(1024)} %bitcast.9) | data formatting | bytes 8192

commit v2 on v1

--- a/solution.py
+++ b/solution.py
@@ -38,9 +38,10 @@
 
 def kernel(
     x_hbm, b_hbm, lab_hbm, don_hbm, mem_hbm, th_hbm, e_hbm, p_hbm,
-    prof_ref, amb_ref, theta_ref, reads_ref,
+    out_ref,
     xs, bs, lab_v, don_v, mem_v, th_v, e_v, p_v, hots, table,
-    send, got, mine, from_core, gene_out, gene_in, final_out, final_in, amb_all, tot_out, tot_in,
+    send, got, mine, from_core, plane_out, plane_in, pair_out, pair_in, z_out, z_in, final_out, final_in,
+    amb_all, tot_out, tot_in,
     in_sem, s_sem, r_sem,
 ):
     d = lax.axis_index("donor")
@@ -63,13 +64,26 @@
         c.start()
 
     barrier = pltpu.get_barrier_semaphore()
-
-    def greet(j, carry):
-        pl.semaphore_signal(barrier, inc=1, device_id={"donor": lax.rem(d + j, 16)}, device_id_type=MESH)
-        pl.semaphore_signal(barrier, inc=1, device_id={"gene": lax.rem(q + 2 * j, 32)}, device_id_type=MESH)
-        return carry
-
-    lax.fori_loop(1, 16, greet, 0)
+    y_hi = lax.rem(q // 2, 2)
+    place = 2 * d + y_hi
+
+    def plane_peer(j):
+        to = lax.rem(place + j, 32)
+        return {"donor": to // 2, "gene": q + 2 * (lax.rem(to, 2) - y_hi)}
+
+    def z_peer(j):
+        return {"gene": lax.rem(q + 4 * j, 32)}
+
+    def greet_z(j, carry):
+        pl.semaphore_signal(barrier, inc=1, device_id=z_peer(j), device_id_type=MESH)
+        return carry
+
+    def greet_plane(j, carry):
+        pl.semaphore_signal(barrier, inc=1, device_id=plane_peer(j), device_id_type=MESH)
+        return carry
+
+    lax.fori_loop(1, 8, greet_z, 0)
+    lax.fori_loop(1, 32, greet_plane, 0)
     pl.semaphore_signal(barrier, inc=1, device_id=other, device_id_type=MESH)
 
     for c in small_in:
@@ -156,7 +170,7 @@
                 send[u // 8, 40 + u % 8 : 40 + u % 8 + run] = turned[64 + r : 64 + r + run]
                 r += run
         if c == 2:
-            pl.semaphore_wait(barrier, 31)
+            pl.semaphore_wait(barrier, 39)
             spread(0, EARLY, 0)
 
     native_row = jnp.sum(native_acc, axis=0, keepdims=True)
@@ -169,115 +183,135 @@
         mine.at[pl.ds(8 - 8 * core, 16)], from_core, s_sem.at[2], r_sem.at[2], device_id=other, device_id_type=MESH
     )
     to_core.start()
-    spread(EARLY, ROWS - EARLY, 1)
+    spread(40, 8, 1)
 
     to_core.wait_recv()
     at_reads = pl.multiple_of(8 * core, 8)
     at_total = pl.multiple_of(8 - 8 * core, 8)
-    gene_out[0:8] = mine[pl.ds(pl.multiple_of(16 * core, 8), 8)] + from_core[pl.ds(at_reads, 8)]
-    gene_out[8:16] = mine[8:16] + from_core[pl.ds(at_total, 8)]
-
-    def to_gene(j, carry):
+    plane_out[...] = jnp.sum(mine[8:16] + from_core[pl.ds(at_total, 8)], axis=0, keepdims=True)
+    pair_out[...] = mine[pl.ds(pl.multiple_of(16 * core, 8), 8)] + from_core[pl.ds(at_reads, 8)]
+
+    def to_plane(j, carry):
         pltpu.make_async_remote_copy(
-            gene_out, gene_in.at[j - 1], s_sem.at[3], r_sem.at[3],
-            device_id={"gene": lax.rem(q + 2 * j, 32)}, device_id_type=MESH,
+            plane_out, plane_in.at[j - 1], s_sem.at[3], r_sem.at[3], device_id=plane_peer(j), device_id_type=MESH
         ).start()
         return carry
 
-    lax.fori_loop(1, 16, to_gene, 0)
+    across = pltpu.make_async_remote_copy(
+        pair_out, pair_in, s_sem.at[4], r_sem.at[4], device_id={"gene": q + 2 - 4 * y_hi}, device_id_type=MESH
+    )
+    across.start()
+    lax.fori_loop(1, 32, to_plane, 0)
+    spread(EARLY, 40 - EARLY, 5)
+
+    across.wait_recv()
+    z_out[...] = pair_out[...] + pair_in[...]
+
+    def to_z(j, carry):
+        pltpu.make_async_remote_copy(
+            z_out, z_in.at[j - 1], s_sem.at[6], r_sem.at[6], device_id=z_peer(j), device_id_type=MESH
+        ).start()
+        return carry
+
+    lax.fori_loop(1, 8, to_z, 0)
 
     def wait_for(ref, sem):
         pltpu.make_async_copy(ref, ref, sem).wait()
 
-    early, late = pl.ds(0, EARLY), pl.ds(EARLY, ROWS - EARLY)
     fifteen = pl.ds(0, 15)
-    wait_for(got.at[fifteen, early], r_sem.at[0])
-    wait_for(got.at[fifteen, late], r_sem.at[1])
-    both = send[d] + jnp.sum(got[...], axis=0)
-    amb_all[d] = both[40:48]
+    wait_for(got.at[fifteen, pl.ds(40, 8)], r_sem.at[1])
+    amb_all[d] = send[d, 40:48] + jnp.sum(got[:, 40:48], axis=0)
 
     def to_all(j, carry):
         pltpu.make_async_remote_copy(
-            amb_all.at[d], amb_all.at[d], s_sem.at[4], r_sem.at[4],
+            amb_all.at[d], amb_all.at[d], s_sem.at[7], r_sem.at[7],
             device_id={"donor": lax.rem(d + j, 16)}, device_id_type=MESH,
         ).start()
         return carry
 
     lax.fori_loop(1, 16, to_all, 0)
 
-    wait_for(gene_in, r_sem.at[3])
-    gene_sum = gene_out[...] + jnp.sum(gene_in[...], axis=0)
-    tot_out[...] = gene_sum[8:16]
-
-    def to_donors(j, carry):
+    wait_for(plane_in, r_sem.at[3])
+    tot_out[...] = plane_out[...] + jnp.sum(plane_in[...], axis=0)
+
+    def total_to_z(j, carry):
         pltpu.make_async_remote_copy(
-            tot_out, tot_in.at[j - 1], s_sem.at[5], r_sem.at[5],
-            device_id={"donor": lax.rem(d + j, 16)}, device_id_type=MESH,
+            tot_out, tot_in.at[j - 1], s_sem.at[8], r_sem.at[8], device_id=z_peer(j), device_id_type=MESH
         ).start()
         return carry
 
-    lax.fori_loop(1, 16, to_donors, 0)
-    final_out[...] = gene_sum[0:8]
+    lax.fori_loop(1, 8, total_to_z, 0)
+
+    wait_for(z_in, r_sem.at[6])
+    final_out[...] = z_out[...] + jnp.sum(z_in[...], axis=0)
     swap = pltpu.make_async_remote_copy(
-        final_out, final_in, s_sem.at[6], r_sem.at[6], device_id=other, device_id_type=MESH
+        final_out, final_in, s_sem.at[9], r_sem.at[9], device_id=other, device_id_type=MESH
     )
     swap.start()
+
+    wait_for(got.at[fifteen, pl.ds(0, EARLY)], r_sem.at[0])
+    wait_for(got.at[fifteen, pl.ds(EARLY, 40 - EARLY)], r_sem.at[5])
+    pop_sums = send[d, 0:40] + jnp.sum(got[:, 0:40], axis=0)
+
     swap.wait_recv()
     ours, theirs = final_out[...], final_in[...]
     native_reads = jnp.where(core == 0, ours, theirs)
     contam_reads = jnp.where(core == 0, theirs, ours)
-    theta_ref[...] = (contam_reads + BETA) / (native_reads + contam_reads + 2.0 * BETA)
-    reads_ref[...] = contam_reads / TOTAL
-
-    wait_for(amb_all.at[fifteen], r_sem.at[4])
-    wait_for(tot_in, r_sem.at[5])
-    total = jnp.sum(tot_out[...] + jnp.sum(tot_in[...], axis=0), axis=0, keepdims=True)
+    out_ref[0:8] = (contam_reads + BETA) / (native_reads + contam_reads + 2.0 * BETA)
+    out_ref[8:16] = contam_reads / TOTAL
+
+    wait_for(amb_all.at[fifteen], r_sem.at[7])
+    ambient = amb_all[...].reshape(128, 128)
+    wait_for(tot_in, r_sem.at[8])
+    total = tot_out[...] + jnp.sum(tot_in[...], axis=0)
 
     def column(wanted, count):
         lanes = lax.broadcasted_iota(jnp.int32, (count, 128), 1)
         rows = lax.broadcasted_iota(jnp.int32, (count, 128), 0)
         return jnp.sum(jnp.where(lanes == wanted(rows), total, 0.0), axis=1, keepdims=True) + TOTAL * PSEUDO
 
-    profile = TOTAL * (both[0:40] + PSEUDO) / column(lambda r: 4 * d + r % 4, 40)
-    below = column(lambda r: POPS + r, DONORS)
-    ambient = amb_all[...].reshape(128, 128)
+    out_ref[16:56] = TOTAL * (pop_sums + PSEUDO) / column(lambda r: 4 * d + r % 4, 40)
+    out_ref[56:184] = TOTAL * (ambient + PSEUDO) / column(lambda r: POPS + r % DONORS, 128)
+
+    wait_for(send.at[fifteen, pl.ds(0, EARLY)], s_sem.at[0])
+    wait_for(send.at[fifteen, pl.ds(40, 8)], s_sem.at[1])
+    wait_for(send.at[fifteen, pl.ds(EARLY, 40 - EARLY)], s_sem.at[5])
+    to_core.wait_send()
+    wait_for(plane_in, s_sem.at[3])
+    across.wait_send()
+    wait_for(z_in, s_sem.at[6])
+    wait_for(amb_all.at[fifteen], s_sem.at[7])
+    wait_for(tot_in, s_sem.at[8])
+    swap.wait_send()
+
+
+def finish(raw_ref, prof_ref, amb_ref, theta_ref, reads_ref):
+    theta_ref[...] = raw_ref[0:8]
+    reads_ref[...] = raw_ref[8:16]
     for t in range(10):
         width = min(128, G - 128 * t)
-        prof_ref[:, 128 * t : 128 * t + width] = profile[4 * t : 4 * t + 4, 0:width]
-        people_rows = TOTAL * (ambient[12 * t : 12 * t + 12] + PSEUDO) / below
-        amb_ref[:, 128 * t : 128 * t + width] = people_rows[:, 0:width]
-
-    wait_for(send.at[fifteen, early], s_sem.at[0])
-    wait_for(send.at[fifteen, late], s_sem.at[1])
-    to_core.wait_send()
-    wait_for(gene_in, s_sem.at[3])
-    wait_for(amb_all.at[fifteen], s_sem.at[4])
-    wait_for(tot_in, s_sem.at[5])
-    swap.wait_send()
+        prof_ref[:, 128 * t : 128 * t + width] = raw_ref[16 + 4 * t : 20 + 4 * t, 0:width]
+        amb_ref[:, 128 * t : 128 * t + width] = raw_ref[56 + 12 * t : 68 + 12 * t, 0:width]
 
 
 def body(tallies, blanks, labels, people, members, theta, profiles, ambient):
     hbm = pl.BlockSpec(memory_space=pltpu.HBM)
     vmem = pl.BlockSpec(memory_space=pltpu.VMEM)
     v = pltpu.VMEM
-    profile, new_ambient, new_theta, reads = pl.pallas_call(
+    raw = pl.pallas_call(
         kernel,
-        out_shape=(
-            jax.ShapeDtypeStruct((4, G), f32),
-            jax.ShapeDtypeStruct((DONORS, G), f32),
-            jax.ShapeDtypeStruct((8, 128), f32),
-            jax.ShapeDtypeStruct((8, 128), f32),
-        ),
+        out_shape=jax.ShapeDtypeStruct((184, 128), f32),
         in_specs=[hbm] * 8,
-        out_specs=(vmem,) * 4,
+        out_specs=vmem,
         scratch_shapes=[
             v((G, N), bf16), v((G, NB), bf16), v((1, N), jnp.int32), v((1, N), jnp.int32),
             v((DONORS, 384), jnp.int32), v((1, N), f32), v((POPS, G), f32), v((DONORS, G), f32),
             v((256, N), bf16), v((256, GP), bf16),
             v((16, ROWS, 128), f32), v((15, ROWS, 128), f32), v((24, 128), f32), v((16, 128), f32),
-            v((16, 128), f32), v((15, 16, 128), f32), v((8, 128), f32), v((8, 128), f32),
-            v((16, 8, 128), f32), v((8, 128), f32), v((15, 8, 128), f32),
-            pltpu.SemaphoreType.DMA((12,)), pltpu.SemaphoreType.DMA((7,)), pltpu.SemaphoreType.DMA((7,)),
+            v((1, 128), f32), v((31, 1, 128), f32), v((8, 128), f32), v((8, 128), f32),
+            v((8, 128), f32), v((7, 8, 128), f32), v((8, 128), f32), v((8, 128), f32),
+            v((16, 8, 128), f32), v((1, 128), f32), v((7, 1, 128), f32),
+            pltpu.SemaphoreType.DMA((12,)), pltpu.SemaphoreType.DMA((10,)), pltpu.SemaphoreType.DMA((10,)),
         ],
         compiler_params=pltpu.CompilerParams(
             collective_id=0, has_side_effects=True, vmem_limit_bytes=56 << 20
@@ -286,6 +320,17 @@
         tallies.T, blanks.T, labels.reshape(1, N), people.reshape(1, N), members, theta.reshape(1, N),
         profiles, ambient,
     )
+    profile, new_ambient, new_theta, reads = pl.pallas_call(
+        finish,
+        out_shape=(
+            jax.ShapeDtypeStruct((4, G), f32),
+            jax.ShapeDtypeStruct((DONORS, G), f32),
+            jax.ShapeDtypeStruct((8, 128), f32),
+            jax.ShapeDtypeStruct((8, 128), f32),
+        ),
+        in_specs=[vmem],
+        out_specs=(vmem,) * 4,
+    )(raw)
     return profile, new_ambient, new_theta.reshape(N), reads.reshape(N)
 
 

time: 42.2 us -> 34.6 us (0.82)
  the two profiles are of different devices: /device:TPU:1 before, /device:TPU:64 now
where the time goes in v2:
time: 34.6 us; the launch traced here: 34.5 us
  Pallas kernels  33.9 us (98%)
  between operations  0.64 us (2%)
    pallas_call x1, Pallas kernels, body(): pl.pallas_call(kernel, out_shape=jax.ShapeDtypeStruct((184, 128), f32), i...  32.3 us
    pallas_call x1, Pallas kernels, body(): pl.pallas_call(finish, out_shape=(jax.ShapeDtypeStruct((4, G), f32), jax....  1.54 us

profile of v2, /device:TPU:64, one launch (start us, length us, event | category | flops | bytes accessed | tf_op | source)
XLA Modules:
  0.0 34.5 jit_solution(7669098545294336892)
XLA Ops:
  0.6 32.3 %shard_map.111.raw_ref = f32[184,128]{1,0:T(8,128)} custom-call(bf16[1261,1024]{1,0:T(8,128)(2,1)} %bitcast.7, bf16[1261,256]{1,0:T(8,128)(2,1)} %bitcast.8, s32[1,1024]{1,0:T(1,128)} %bitcast.9, s32[1,1024]{1,0:T(1,128)} %bitcast.10, s32[12,384]{1,0:T(8,128)} %mem_hbm.1, f32[1,1024]{1,0:T(1,128)} %bitcast.11, f32[64,1261]{1,0:T(8,128)} %e_hbm.1, ...), custom_call_target="tpu_custom_call" | custom-call | tf_op jit(solution)/shard_map/pallas_call | solution.py:301
  33.0 1.5 %shard_map.112 = (f32[4,1261]{1,0:T(4,128)}, f32[12,1261]{1,0:T(8,128)}, f32[8,128]{1,0:T(8,128)}, f32[8,128]{1,0:T(8,128)}) custom-call(f32[184,128]{1,0:T(8,128)} %shard_map.111.raw_ref), custom_call_target="tpu_custom_call" | custom-call | tf_op jit(solution)/shard_map/pallas_call | solution.py:323

commit v3 on v2

--- a/solution.py
+++ b/solution.py
@@ -11,8 +11,7 @@
 G, N, NB, GP = 1261, 1024, 256, 1280
 POPS, DONORS = 64, 12
 CHUNK = 256
-EARLY = 24
-ROWS = 48
+EARLY = 3
 f32, bf16 = jnp.float32, jnp.bfloat16
 MESH = pl.DeviceIdType.MESH
 LAST = (((1,), (1,)), ((), ()))
@@ -40,8 +39,8 @@
     x_hbm, b_hbm, lab_hbm, don_hbm, mem_hbm, th_hbm, e_hbm, p_hbm,
     out_ref,
     xs, bs, lab_v, don_v, mem_v, th_v, e_v, p_v, hots, table,
-    send, got, mine, from_core, plane_out, plane_in, pair_out, pair_in, z_out, z_in, final_out, final_in,
-    amb_all, tot_out, tot_in,
+    pop_send, x_got, y_send, y_got, amb_send, amb_got, amb_all, mine, from_core, pair_out, pair_in, z_out, z_in,
+    plane_out, plane_in, tot_out, tot_in,
     in_sem, s_sem, r_sem,
 ):
     d = lax.axis_index("donor")
@@ -71,20 +70,28 @@
         to = lax.rem(place + j, 32)
         return {"donor": to // 2, "gene": q + 2 * (lax.rem(to, 2) - y_hi)}
 
+    spot = 2 * (q // 4) + core
+
     def z_peer(j):
-        return {"gene": lax.rem(q + 4 * j, 32)}
-
-    def greet_z(j, carry):
-        pl.semaphore_signal(barrier, inc=1, device_id=z_peer(j), device_id_type=MESH)
-        return carry
-
-    def greet_plane(j, carry):
-        pl.semaphore_signal(barrier, inc=1, device_id=plane_peer(j), device_id_type=MESH)
-        return carry
-
-    lax.fori_loop(1, 8, greet_z, 0)
-    lax.fori_loop(1, 32, greet_plane, 0)
-    pl.semaphore_signal(barrier, inc=1, device_id=other, device_id_type=MESH)
+        to = lax.rem(spot + j, 16)
+        return {"gene": 4 * (to // 2) + 2 * y_hi + lax.rem(to, 2)}
+
+    def far_first(i, middle):
+        return middle + (i + 1) // 2 * (1 - 2 * lax.rem(i, 2))
+
+    def signal_to(peer):
+        pl.semaphore_signal(barrier, inc=1, device_id=peer, device_id_type=MESH)
+
+    def greet_z(i, carry):
+        signal_to(z_peer(far_first(i, 8)))
+        return carry
+
+    def greet_plane(i, carry):
+        signal_to(plane_peer(far_first(i, 16)))
+        return carry
+
+    lax.fori_loop(0, 15, greet_z, 0)
+    lax.fori_loop(0, 31, greet_plane, 0)
 
     for c in small_in:
         c.wait()
@@ -119,30 +126,41 @@
     listed_hi = listed.astype(bf16)
     listed_lo = (listed - listed_hi.astype(f32)).astype(bf16)
 
+    listed_both = jnp.concatenate([listed_hi, listed_lo], axis=1)
     pops = jnp.concatenate([pop_hot, jnp.zeros((64, N), bf16)], axis=0)
     folk = jnp.concatenate([jnp.zeros((64, N), bf16), donor_hot, jnp.zeros((48, N), bf16)], axis=0)
-    send[15, 40:48] = jnp.zeros((8, 128), f32)
+    amb_send[15] = jnp.zeros((8, 128), f32)
 
     native_acc = jnp.zeros((8, N), f32)
     contam_acc = jnp.zeros((8, N), f32)
     totals = jnp.zeros((8, 128), f32)
 
-    def spread(first, count, index):
-        def one(j, carry):
-            peer = lax.rem(d + j, 16)
-            pltpu.make_async_remote_copy(
-                send.at[peer, pl.ds(first, count)], got.at[j - 1, pl.ds(first, count)],
-                s_sem.at[index], r_sem.at[index], device_id={"donor": peer}, device_id_type=MESH,
-            ).start()
-            return carry
-
-        lax.fori_loop(1, 16, one, 0)
-
+    x_at, y_at = d // 4, lax.rem(d, 4)
+
+    def to_x(first, count, index):
+        copies = []
+        for j in (2, 1, 3):
+            there = lax.rem(x_at + j, 4)
+            copies.append(
+                pltpu.make_async_remote_copy(
+                    pop_send.at[there, pl.ds(first, count)], x_got.at[j - 1, pl.ds(first, count)],
+                    s_sem.at[index], r_sem.at[index], device_id={"donor": 4 * there + y_at}, device_id_type=MESH,
+                )
+            )
+            copies[-1].start()
+        return copies
+
+    def look_up(c):
+        part = table[:, CHUNK * c : CHUNK * c + CHUNK]
+        return lax.dot_general(part, hots[...], FIRST, preferred_element_type=f32)
+
+    for c in x_in[:EARLY] + [b_in]:
+        c.wait()
+    ahead = look_up(0)
     for c in range(5):
-        log_odds = lax.dot_general(table[:, CHUNK * c : CHUNK * c + CHUNK], hots[...], FIRST, preferred_element_type=f32)
-        x_in[c].wait()
-        if c == 0:
-            b_in.wait()
+        log_odds = ahead
+        if c < 4:
+            ahead = look_up(c + 1)
         if c < 4:
             counts, blanks = xs[CHUNK * c : CHUNK * c + CHUNK], bs[CHUNK * c : CHUNK * c + CHUNK]
         else:
@@ -155,72 +173,92 @@
         contam_acc = contam_acc + jnp.sum(contam.astype(f32).reshape(CHUNK // 8, 8, N), axis=0)
         sums = lax.dot_general(native, pops, LAST, preferred_element_type=f32)
         sums = sums + lax.dot_general(contam, folk, LAST, preferred_element_type=f32)
-        sums = sums + jnp.dot(blanks, listed_hi, preferred_element_type=f32)
-        sums = sums + jnp.dot(blanks, listed_lo, preferred_element_type=f32)
+        extra = jnp.dot(blanks, listed_both, preferred_element_type=f32)
+        sums = sums + (extra[:, 0:128] + extra[:, 128:256])
         totals = totals + jnp.sum(sums.reshape(CHUNK // 8, 8, 128), axis=0)
         for h in range(2):
             t = 2 * c + h
             turned = sums[128 * h : 128 * h + 128].T
             for i in range(16):
-                send[i, 4 * t : 4 * t + 4] = turned[4 * i : 4 * i + 4]
+                pop_send[i // 4, c, i % 4, 4 * h : 4 * h + 4] = turned[4 * i : 4 * i + 4]
             r = 0
             while r < DONORS:
                 u = 12 * t + r
                 run = min(DONORS - r, 8 - u % 8)
-                send[u // 8, 40 + u % 8 : 40 + u % 8 + run] = turned[64 + r : 64 + r + run]
+                amb_send[u // 8, u % 8 : u % 8 + run] = turned[64 + r : 64 + r + run]
                 r += run
-        if c == 2:
-            pl.semaphore_wait(barrier, 39)
-            spread(0, EARLY, 0)
-
+        if c == EARLY - 1:
+            pl.semaphore_wait(barrier, 46)
+            to_x(0, EARLY, 0)
+            for e in x_in[EARLY:]:
+                e.wait()
+
+    plane_out[...] = jnp.sum(totals, axis=0, keepdims=True)
     native_row = jnp.sum(native_acc, axis=0, keepdims=True)
     contam_row = jnp.sum(contam_acc, axis=0, keepdims=True)
     for i in range(8):
-        mine[i : i + 1] = native_row[:, 128 * i : 128 * i + 128]
-        mine[16 + i : 17 + i] = contam_row[:, 128 * i : 128 * i + 128]
-    mine[8:16] = totals
+        mine[0, i : i + 1] = native_row[:, 128 * i : 128 * i + 128]
+        mine[1, i : i + 1] = contam_row[:, 128 * i : 128 * i + 128]
     to_core = pltpu.make_async_remote_copy(
-        mine.at[pl.ds(8 - 8 * core, 16)], from_core, s_sem.at[2], r_sem.at[2], device_id=other, device_id_type=MESH
+        mine.at[1 - core], from_core, s_sem.at[2], r_sem.at[2], device_id=other, device_id_type=MESH
     )
     to_core.start()
-    spread(40, 8, 1)
-
+
+    def to_plane(i, carry):
+        j = far_first(i, 16)
+        pltpu.make_async_remote_copy(
+            plane_out, plane_in.at[j - 1], s_sem.at[3], r_sem.at[3], device_id=plane_peer(j), device_id_type=MESH
+        ).start()
+        return carry
+
+    lax.fori_loop(0, 31, to_plane, 0)
     to_core.wait_recv()
-    at_reads = pl.multiple_of(8 * core, 8)
-    at_total = pl.multiple_of(8 - 8 * core, 8)
-    plane_out[...] = jnp.sum(mine[8:16] + from_core[pl.ds(at_total, 8)], axis=0, keepdims=True)
-    pair_out[...] = mine[pl.ds(pl.multiple_of(16 * core, 8), 8)] + from_core[pl.ds(at_reads, 8)]
-
-    def to_plane(j, carry):
-        pltpu.make_async_remote_copy(
-            plane_out, plane_in.at[j - 1], s_sem.at[3], r_sem.at[3], device_id=plane_peer(j), device_id_type=MESH
-        ).start()
-        return carry
-
+    pair_out[...] = mine[core] + from_core[...]
     across = pltpu.make_async_remote_copy(
         pair_out, pair_in, s_sem.at[4], r_sem.at[4], device_id={"gene": q + 2 - 4 * y_hi}, device_id_type=MESH
     )
     across.start()
-    lax.fori_loop(1, 32, to_plane, 0)
-    spread(EARLY, 40 - EARLY, 5)
+
+    def to_owner(j, carry):
+        peer = lax.rem(d + j, 16)
+        pltpu.make_async_remote_copy(
+            amb_send.at[peer], amb_got.at[j - 1], s_sem.at[1], r_sem.at[1],
+            device_id={"donor": peer}, device_id_type=MESH,
+        ).start()
+        return carry
+
+    lax.fori_loop(1, 16, to_owner, 0)
+    to_x(EARLY, 5 - EARLY, 5)
 
     across.wait_recv()
     z_out[...] = pair_out[...] + pair_in[...]
 
-    def to_z(j, carry):
+    def to_z(i, carry):
+        j = far_first(i, 8)
         pltpu.make_async_remote_copy(
             z_out, z_in.at[j - 1], s_sem.at[6], r_sem.at[6], device_id=z_peer(j), device_id_type=MESH
         ).start()
         return carry
 
-    lax.fori_loop(1, 8, to_z, 0)
+    lax.fori_loop(0, 15, to_z, 0)
 
     def wait_for(ref, sem):
         pltpu.make_async_copy(ref, ref, sem).wait()
 
-    fifteen = pl.ds(0, 15)
-    wait_for(got.at[fifteen, pl.ds(40, 8)], r_sem.at[1])
-    amb_all[d] = send[d, 40:48] + jnp.sum(got[:, 40:48], axis=0)
+    wait_for(plane_in, r_sem.at[3])
+    tot_out[...] = plane_out[...] + jnp.sum(plane_in[...], axis=0)
+
+    def total_to_z(i, carry):
+        j = far_first(i, 8)
+        pltpu.make_async_remote_copy(
+            tot_out, tot_in.at[j - 1], s_sem.at[8], r_sem.at[8], device_id=z_peer(j), device_id_type=MESH
+        ).start()
+        return carry
+
+    lax.fori_loop(0, 15, total_to_z, 0)
+
+    wait_for(amb_got, r_sem.at[1])
+    amb_all[d] = amb_send[d] + jnp.sum(amb_got[...], axis=0)
 
     def to_all(j, carry):
         pltpu.make_async_remote_copy(
@@ -231,36 +269,36 @@
 
     lax.fori_loop(1, 16, to_all, 0)
 
-    wait_for(plane_in, r_sem.at[3])
-    tot_out[...] = plane_out[...] + jnp.sum(plane_in[...], axis=0)
-
-    def total_to_z(j, carry):
-        pltpu.make_async_remote_copy(
-            tot_out, tot_in.at[j - 1], s_sem.at[8], r_sem.at[8], device_id=z_peer(j), device_id_type=MESH
-        ).start()
-        return carry
-
-    lax.fori_loop(1, 8, total_to_z, 0)
+    three = pl.ds(0, 3)
+    wait_for(x_got.at[three, pl.ds(0, EARLY)], r_sem.at[0])
+    wait_for(x_got.at[three, pl.ds(EARLY, 5 - EARLY)], r_sem.at[5])
+    y_send[...] = pop_send[x_at] + jnp.sum(x_got[...], axis=0)
+    to_y = []
+    for j in (2, 1, 3):
+        there = lax.rem(y_at + j, 4)
+        to_y.append(
+            pltpu.make_async_remote_copy(
+                y_send.at[:, there], y_got.at[j - 1], s_sem.at[9], r_sem.at[9],
+                device_id={"donor": 4 * x_at + there}, device_id_type=MESH,
+            )
+        )
+        to_y[-1].start()
 
     wait_for(z_in, r_sem.at[6])
-    final_out[...] = z_out[...] + jnp.sum(z_in[...], axis=0)
-    swap = pltpu.make_async_remote_copy(
-        final_out, final_in, s_sem.at[9], r_sem.at[9], device_id=other, device_id_type=MESH
-    )
-    swap.start()
-
-    wait_for(got.at[fifteen, pl.ds(0, EARLY)], r_sem.at[0])
-    wait_for(got.at[fifteen, pl.ds(EARLY, 40 - EARLY)], r_sem.at[5])
-    pop_sums = send[d, 0:40] + jnp.sum(got[:, 0:40], axis=0)
-
-    swap.wait_recv()
-    ours, theirs = final_out[...], final_in[...]
+    ours, theirs = z_out[...], z_in[0]
+    for j in range(2, 16):
+        if j % 2:
+            theirs = theirs + z_in[j - 1]
+        else:
+            ours = ours + z_in[j - 1]
     native_reads = jnp.where(core == 0, ours, theirs)
     contam_reads = jnp.where(core == 0, theirs, ours)
     out_ref[0:8] = (contam_reads + BETA) / (native_reads + contam_reads + 2.0 * BETA)
     out_ref[8:16] = contam_reads / TOTAL
 
-    wait_for(amb_all.at[fifteen], r_sem.at[7])
+    wait_for(y_got, r_sem.at[9])
+    pop_sums = (y_send[:, y_at] + jnp.sum(y_got[...], axis=0)).reshape(40, 128)
+    wait_for(amb_all.at[pl.ds(0, 15)], r_sem.at[7])
     ambient = amb_all[...].reshape(128, 128)
     wait_for(tot_in, r_sem.at[8])
     total = tot_out[...] + jnp.sum(tot_in[...], axis=0)
@@ -273,16 +311,16 @@
     out_ref[16:56] = TOTAL * (pop_sums + PSEUDO) / column(lambda r: 4 * d + r % 4, 40)
     out_ref[56:184] = TOTAL * (ambient + PSEUDO) / column(lambda r: POPS + r % DONORS, 128)
 
-    wait_for(send.at[fifteen, pl.ds(0, EARLY)], s_sem.at[0])
-    wait_for(send.at[fifteen, pl.ds(40, 8)], s_sem.at[1])
-    wait_for(send.at[fifteen, pl.ds(EARLY, 40 - EARLY)], s_sem.at[5])
+    wait_for(x_got.at[three, pl.ds(0, EARLY)], s_sem.at[0])
+    wait_for(x_got.at[three, pl.ds(EARLY, 5 - EARLY)], s_sem.at[5])
+    wait_for(amb_got, s_sem.at[1])
     to_core.wait_send()
     wait_for(plane_in, s_sem.at[3])
     across.wait_send()
     wait_for(z_in, s_sem.at[6])
-    wait_for(amb_all.at[fifteen], s_sem.at[7])
+    wait_for(amb_all.at[pl.ds(0, 15)], s_sem.at[7])
     wait_for(tot_in, s_sem.at[8])
-    swap.wait_send()
+    wait_for(y_got, s_sem.at[9])
 
 
 def finish(raw_ref, prof_ref, amb_ref, theta_ref, reads_ref):
@@ -307,10 +345,10 @@
             v((G, N), bf16), v((G, NB), bf16), v((1, N), jnp.int32), v((1, N), jnp.int32),
             v((DONORS, 384), jnp.int32), v((1, N), f32), v((POPS, G), f32), v((DONORS, G), f32),
             v((256, N), bf16), v((256, GP), bf16),
-            v((16, ROWS, 128), f32), v((15, ROWS, 128), f32), v((24, 128), f32), v((16, 128), f32),
-            v((1, 128), f32), v((31, 1, 128), f32), v((8, 128), f32), v((8, 128), f32),
-            v((8, 128), f32), v((7, 8, 128), f32), v((8, 128), f32), v((8, 128), f32),
-            v((16, 8, 128), f32), v((1, 128), f32), v((7, 1, 128), f32),
+            v((4, 5, 4, 8, 128), f32), v((3, 5, 4, 8, 128), f32), v((5, 4, 8, 128), f32), v((3, 5, 8, 128), f32),
+            v((16, 8, 128), f32), v((15, 8, 128), f32), v((16, 8, 128), f32),
+            v((2, 8, 128), f32), v((8, 128), f32), v((8, 128), f32), v((8, 128), f32), v((8, 128), f32),
+            v((15, 8, 128), f32), v((1, 128), f32), v((31, 1, 128), f32), v((1, 128), f32), v((15, 1, 128), f32),
             pltpu.SemaphoreType.DMA((12,)), pltpu.SemaphoreType.DMA((10,)), pltpu.SemaphoreType.DMA((10,)),
         ],
         compiler_params=pltpu.CompilerParams(

time: 34.6 us -> 31.6 us (0.913)
  the two profiles are of different devices: /device:TPU:64 before, /device:TPU:1 now
where the time goes in v3:
time: 31.6 us; the launch traced here: 31.4 us
  Pallas kernels  30.8 us (97%)
  between operations  0.64 us (2%)
    pallas_call x1, Pallas kernels, body(): pl.pallas_call(kernel, out_shape=jax.ShapeDtypeStruct((184, 128), f32), i...  29.2 us
    pallas_call x1, Pallas kernels, body(): pl.pallas_call(finish, out_shape=(jax.ShapeDtypeStruct((4, G), f32), jax....  1.54 us

profile of v3, /device:TPU:1, one launch (start us, length us, event | category | flops | bytes accessed | tf_op | source)
XLA Modules:
  0.0 31.4 jit_solution(6259261129971625355)
XLA Ops:
  0.6 29.2 %shard_map.111.raw_ref = f32[184,128]{1,0:T(8,128)} custom-call(bf16[1261,1024]{1,0:T(8,128)(2,1)} %bitcast.7, bf16[1261,256]{1,0:T(8,128)(2,1)} %bitcast.8, s32[1,1024]{1,0:T(1,128)} %bitcast.9, s32[1,1024]{1,0:T(1,128)} %bitcast.10, s32[12,384]{1,0:T(8,128)} %mem_hbm.1, f32[1,1024]{1,0:T(1,128)} %bitcast.11, f32[64,1261]{1,0:T(8,128)} %e_hbm.1, ...), custom_call_target="tpu_custom_call" | custom-call | tf_op jit(solution)/shard_map/pallas_call | solution.py:339
  29.9 1.5 %shard_map.112 = (f32[4,1261]{1,0:T(4,128)}, f32[12,1261]{1,0:T(8,128)}, f32[8,128]{1,0:T(8,128)}, f32[8,128]{1,0:T(8,128)}) custom-call(f32[184,128]{1,0:T(8,128)} %shard_map.111.raw_ref), custom_call_target="tpu_custom_call" | custom-call | tf_op jit(solution)/shard_map/pallas_call | solution.py:361

commit v4 on v3

--- a/solution.py
+++ b/solution.py
@@ -90,8 +90,8 @@
         signal_to(plane_peer(far_first(i, 16)))
         return carry
 
+    lax.fori_loop(0, 31, greet_plane, 0)
     lax.fori_loop(0, 15, greet_z, 0)
-    lax.fori_loop(0, 31, greet_plane, 0)
 
     for c in small_in:
         c.wait()
@@ -154,7 +154,7 @@
         part = table[:, CHUNK * c : CHUNK * c + CHUNK]
         return lax.dot_general(part, hots[...], FIRST, preferred_element_type=f32)
 
-    for c in x_in[:EARLY] + [b_in]:
+    for c in x_in + [b_in]:
         c.wait()
     ahead = look_up(0)
     for c in range(5):
@@ -187,13 +187,18 @@
                 run = min(DONORS - r, 8 - u % 8)
                 amb_send[u // 8, u % 8 : u % 8 + run] = turned[64 + r : 64 + r + run]
                 r += run
-        if c == EARLY - 1:
-            pl.semaphore_wait(barrier, 46)
-            to_x(0, EARLY, 0)
-            for e in x_in[EARLY:]:
-                e.wait()
 
     plane_out[...] = jnp.sum(totals, axis=0, keepdims=True)
+    pl.semaphore_wait(barrier, 46)
+
+    def to_plane(i, carry):
+        j = far_first(i, 16)
+        pltpu.make_async_remote_copy(
+            plane_out, plane_in.at[j - 1], s_sem.at[3], r_sem.at[3], device_id=plane_peer(j), device_id_type=MESH
+        ).start()
+        return carry
+
+    lax.fori_loop(0, 31, to_plane, 0)
     native_row = jnp.sum(native_acc, axis=0, keepdims=True)
     contam_row = jnp.sum(contam_acc, axis=0, keepdims=True)
     for i in range(8):
@@ -204,14 +209,8 @@
     )
     to_core.start()
 
-    def to_plane(i, carry):
-        j = far_first(i, 16)
-        pltpu.make_async_remote_copy(
-            plane_out, plane_in.at[j - 1], s_sem.at[3], r_sem.at[3], device_id=plane_peer(j), device_id_type=MESH
-        ).start()
-        return carry
-
-    lax.fori_loop(0, 31, to_plane, 0)
+    to_x(0, EARLY, 0)
+    to_x(EARLY, 5 - EARLY, 5)
     to_core.wait_recv()
     pair_out[...] = mine[core] + from_core[...]
     across = pltpu.make_async_remote_copy(
@@ -228,7 +227,6 @@
         return carry
 
     lax.fori_loop(1, 16, to_owner, 0)
-    to_x(EARLY, 5 - EARLY, 5)
 
     across.wait_recv()
     z_out[...] = pair_out[...] + pair_in[...]

time: 31.6 us -> 31 us (0.981)
  Pallas kernels: 30.8 us -> 30.2 us
    pallas_call x1, Pallas kernels: 29.2 us -> 28.7 us  [body(): pl.pallas_call(kernel, out_shape=jax.ShapeDtypeStruct((184, 128), f32), i...]
where the time goes in v4:
time: 31 us; the launch traced here: 30.9 us
  Pallas kernels  30.2 us (97%)
  between operations  0.64 us (2%)
    pallas_call x1, Pallas kernels, body(): pl.pallas_call(kernel, out_shape=jax.ShapeDtypeStruct((184, 128), f32), i...  28.7 us
    pallas_call x1, Pallas kernels, body(): pl.pallas_call(finish, out_shape=(jax.ShapeDtypeStruct((4, G), f32), jax....  1.54 us

profile of v4, /device:TPU:1, one launch (start us, length us, event | category | flops | bytes accessed | tf_op | source)
XLA Modules:
  0.0 30.9 jit_solution(18216943133952190652)
XLA Ops:
  0.6 28.7 %shard_map.111.raw_ref = f32[184,128]{1,0:T(8,128)} custom-call(bf16[1261,1024]{1,0:T(8,128)(2,1)} %bitcast.7, bf16[1261,256]{1,0:T(8,128)(2,1)} %bitcast.8, s32[1,1024]{1,0:T(1,128)} %bitcast.9, s32[1,1024]{1,0:T(1,128)} %bitcast.10, s32[12,384]{1,0:T(8,128)} %mem_hbm.1, f32[1,1024]{1,0:T(1,128)} %bitcast.11, f32[64,1261]{1,0:T(8,128)} %e_hbm.1, ...), custom_call_target="tpu_custom_call" | custom-call | tf_op jit(solution)/shard_map/pallas_call | solution.py:337
  29.3 1.5 %shard_map.112 = (f32[4,1261]{1,0:T(4,128)}, f32[12,1261]{1,0:T(8,128)}, f32[8,128]{1,0:T(8,128)}, f32[8,128]{1,0:T(8,128)}) custom-call(f32[184,128]{1,0:T(8,128)} %shard_map.111.raw_ref), custom_call_target="tpu_custom_call" | custom-call | tf_op jit(solution)/shard_map/pallas_call | solution.py:359

commit v5 on v4

--- a/solution.py
+++ b/solution.py
@@ -54,13 +54,10 @@
     small_in = [pltpu.make_async_copy(a, b, in_sem.at[i]) for i, (a, b) in enumerate(smalls)]
     for c in small_in:
         c.start()
-    x_in = []
-    for c in range(5):
-        rows = pl.ds(CHUNK * c, min(CHUNK, G - CHUNK * c))
-        x_in.append(pltpu.make_async_copy(x_hbm.at[rows], xs.at[rows], in_sem.at[6 + c]))
-    b_in = pltpu.make_async_copy(b_hbm, bs, in_sem.at[11])
-    for c in x_in[:1] + [b_in] + x_in[1:]:
-        c.start()
+    x_in = pltpu.make_async_copy(x_hbm, xs, in_sem.at[6])
+    b_in = pltpu.make_async_copy(b_hbm, bs, in_sem.at[7])
+    x_in.start()
+    b_in.start()
 
     barrier = pltpu.get_barrier_semaphore()
     y_hi = lax.rem(q // 2, 2)
@@ -77,7 +74,7 @@
         return {"gene": 4 * (to // 2) + 2 * y_hi + lax.rem(to, 2)}
 
     def far_first(i, middle):
-        return middle + (i + 1) // 2 * (1 - 2 * lax.rem(i, 2))
+        return middle + (i + 1) // 2 * (1 - 2 * (i % 2))
 
     def signal_to(peer):
         pl.semaphore_signal(barrier, inc=1, device_id=peer, device_id_type=MESH)
@@ -90,8 +87,10 @@
         signal_to(plane_peer(far_first(i, 16)))
         return carry
 
-    lax.fori_loop(0, 31, greet_plane, 0)
-    lax.fori_loop(0, 15, greet_z, 0)
+    for i in range(31):
+        greet_plane(i, 0)
+    for i in range(15):
+        greet_z(i, 0)
 
     for c in small_in:
         c.wait()
@@ -115,14 +114,17 @@
     table[0:240, G:GP] = jnp.zeros((240, GP - G), bf16)
 
     members = mem_v[...] - d * NB
-    empties = lax.broadcasted_iota(jnp.int32, (NB, 128), 0)
+    here = (members >= 0) & (members < NB)
+    members = jnp.where(here, members, -1).astype(f32).astype(bf16)
+    empties = lax.broadcasted_iota(jnp.int32, (NB, 128), 0).astype(f32).astype(bf16)
+    one, none = jnp.ones((NB, 128), bf16), jnp.zeros((NB, 128), bf16)
     lane = lax.broadcasted_iota(jnp.int32, (128, 128), 1)
     listed = jnp.zeros((NB, 128), f32)
     for r in range(DONORS):
-        count = jnp.zeros((NB, 128), f32)
+        count = none
         for t in range(3):
-            count = count + jnp.where(members[r : r + 1, 128 * t : 128 * t + 128] == empties, 1.0, 0.0)
-        listed = listed + jnp.dot(count.astype(bf16), hot(lane == POPS + r), preferred_element_type=f32)
+            count = count + jnp.where(members[r : r + 1, 128 * t : 128 * t + 128] == empties, one, none)
+        listed = listed + jnp.dot(count, hot(lane == POPS + r), preferred_element_type=f32)
     listed_hi = listed.astype(bf16)
     listed_lo = (listed - listed_hi.astype(f32)).astype(bf16)
 
@@ -154,8 +156,8 @@
         part = table[:, CHUNK * c : CHUNK * c + CHUNK]
         return lax.dot_general(part, hots[...], FIRST, preferred_element_type=f32)
 
-    for c in x_in + [b_in]:
-        c.wait()
+    x_in.wait()
+    b_in.wait()
     ahead = look_up(0)
     for c in range(5):
         log_odds = ahead
@@ -198,7 +200,8 @@
         ).start()
         return carry
 
-    lax.fori_loop(0, 31, to_plane, 0)
+    for i in range(31):
+        to_plane(i, 0)
     native_row = jnp.sum(native_acc, axis=0, keepdims=True)
     contam_row = jnp.sum(contam_acc, axis=0, keepdims=True)
     for i in range(8):
@@ -253,7 +256,8 @@
         ).start()
         return carry
 
-    lax.fori_loop(0, 15, total_to_z, 0)
+    for i in range(15):
+        total_to_z(i, 0)
 
     wait_for(amb_got, r_sem.at[1])
     amb_all[d] = amb_send[d] + jnp.sum(amb_got[...], axis=0)
@@ -298,17 +302,8 @@
     pop_sums = (y_send[:, y_at] + jnp.sum(y_got[...], axis=0)).reshape(40, 128)
     wait_for(amb_all.at[pl.ds(0, 15)], r_sem.at[7])
     ambient = amb_all[...].reshape(128, 128)
-    wait_for(tot_in, r_sem.at[8])
-    total = tot_out[...] + jnp.sum(tot_in[...], axis=0)
-
-    def column(wanted, count):
-        lanes = lax.broadcasted_iota(jnp.int32, (count, 128), 1)
-        rows = lax.broadcasted_iota(jnp.int32, (count, 128), 0)
-        return jnp.sum(jnp.where(lanes == wanted(rows), total, 0.0), axis=1, keepdims=True) + TOTAL * PSEUDO
-
-    out_ref[16:56] = TOTAL * (pop_sums + PSEUDO) / column(lambda r: 4 * d + r % 4, 40)
-    out_ref[56:184] = TOTAL * (ambient + PSEUDO) / column(lambda r: POPS + r % DONORS, 128)
-
+    over_pops = TOTAL * (pop_sums + PSEUDO)
+    over_ambient = TOTAL * (ambient + PSEUDO)
     wait_for(x_got.at[three, pl.ds(0, EARLY)], s_sem.at[0])
     wait_for(x_got.at[three, pl.ds(EARLY, 5 - EARLY)], s_sem.at[5])
     wait_for(amb_got, s_sem.at[1])
@@ -317,8 +312,22 @@
     across.wait_send()
     wait_for(z_in, s_sem.at[6])
     wait_for(amb_all.at[pl.ds(0, 15)], s_sem.at[7])
+    wait_for(y_got, s_sem.at[9])
+    wait_for(tot_in, r_sem.at[8])
+    total = tot_out[...] + jnp.sum(tot_in[...], axis=0)
+
+    def column(wanted, count):
+        lanes = lax.broadcasted_iota(jnp.int32, (count, 128), 1)
+        rows = lax.broadcasted_iota(jnp.int32, (count, 128), 0)
+        return jnp.sum(jnp.where(lanes == wanted(rows), total, 0.0), axis=1, keepdims=True) + TOTAL * PSEUDO
+
+    pop_column = column(lambda r: 4 * d + r % 4, 8)
+    out_ref[16:56] = (over_pops.reshape(5, 8, 128) / pop_column[None]).reshape(40, 128)
+    ambient_column = column(lambda r: POPS + r % DONORS, 24)
+    for k in range(0, 128, 24):
+        rows = min(24, 128 - k)
+        out_ref[56 + k : 56 + k + rows] = over_ambient[k : k + rows] / ambient_column[0:rows]
     wait_for(tot_in, s_sem.at[8])
-    wait_for(y_got, s_sem.at[9])
 
 
 def finish(raw_ref, prof_ref, amb_ref, theta_ref, reads_ref):
@@ -347,7 +356,7 @@
             v((16, 8, 128), f32), v((15, 8, 128), f32), v((16, 8, 128), f32),
             v((2, 8, 128), f32), v((8, 128), f32), v((8, 128), f32), v((8, 128), f32), v((8, 128), f32),
             v((15, 8, 128), f32), v((1, 128), f32), v((31, 1, 128), f32), v((1, 128), f32), v((15, 1, 128), f32),
-            pltpu.SemaphoreType.DMA((12,)), pltpu.SemaphoreType.DMA((10,)), pltpu.SemaphoreType.DMA((10,)),
+            pltpu.SemaphoreType.DMA((8,)), pltpu.SemaphoreType.DMA((10,)), pltpu.SemaphoreType.DMA((10,)),
         ],
         compiler_params=pltpu.CompilerParams(
             collective_id=0, has_side_effects=True, vmem_limit_bytes=56 << 20

time: 31 us -> 30.4 us (0.981)
  Pallas kernels: 30.2 us -> 29.6 us
    pallas_call x1, Pallas kernels: 28.7 us -> 28 us  [body(): pl.pallas_call(kernel, out_shape=jax.ShapeDtypeStruct((184, 128), f32), i...]
where the time goes in v5:
time: 30.4 us; the launch traced here: 30.2 us
  Pallas kernels  29.6 us (97%)
  between operations  0.64 us (2%)
    pallas_call x1, Pallas kernels, body(): pl.pallas_call(kernel, out_shape=jax.ShapeDtypeStruct((184, 128), f32), i...  28 us
    pallas_call x1, Pallas kernels, body(): pl.pallas_call(finish, out_shape=(jax.ShapeDtypeStruct((4, G), f32), jax....  1.54 us

profile of v5, /device:TPU:1, one launch (start us, length us, event | category | flops | bytes accessed | tf_op | source)
XLA Modules:
  0.0 30.2 jit_solution(8619029312375162989)
XLA Ops:
  0.6 28.0 %shard_map.111.raw_ref = f32[184,128]{1,0:T(8,128)} custom-call(bf16[1261,1024]{1,0:T(8,128)(2,1)} %bitcast.7, bf16[1261,256]{1,0:T(8,128)(2,1)} %bitcast.8, s32[1,1024]{1,0:T(1,128)} %bitcast.9, s32[1,1024]{1,0:T(1,128)} %bitcast.10, s32[12,384]{1,0:T(8,128)} %mem_hbm.1, f32[1,1024]{1,0:T(1,128)} %bitcast.11, f32[64,1261]{1,0:T(8,128)} %e_hbm.1, ...), custom_call_target="tpu_custom_call" | custom-call | tf_op jit(solution)/shard_map/pallas_call | solution.py:346
  28.7 1.5 %shard_map.112 = (f32[4,1261]{1,0:T(4,128)}, f32[12,1261]{1,0:T(8,128)}, f32[8,128]{1,0:T(8,128)}, f32[8,128]{1,0:T(8,128)}) custom-call(f32[184,128]{1,0:T(8,128)} %shard_map.111.raw_ref), custom_call_target="tpu_custom_call" | custom-call | tf_op jit(solution)/shard_map/pallas_call | solution.py:368
